TPU v7x, 512 devices: a whole 4x8x8 slice. The times are simulated.
512 devices in a mesh: wide: 64 (over y, x, z_lo), narrow: 8 (over z_hi, core).
Axes of the slice: x: 4, y: 8, z: 8 (z_hi: 4, z_lo: 2; z = z_hi * 2 + z_lo), core: 2. Of those that a mesh axis runs over, the one named last changes fastest.
Arguments:
- tval: bfloat16 [4096, 12, 128, 128], P(('wide', 'narrow')), may hold values from -0.16992188 to 0.16992188
- tcol: int32 [4096, 12], replicated, may hold values from 0 to 4095, as said below
- ocol: int32 [4096, 12], P(('wide', 'narrow')), may hold values from 0 to 4095, as said below
- basis: bfloat16 [524288, 128], P(('wide', 'narrow')), may hold values from -6 to 6
Outputs:
- projected: bfloat16 [524288, 128], P(('wide', 'narrow'))
- level: float32 [128, 128], replicated
Inputs may be any that keep to these rules, and one draw needn't show every extreme that they name: `tcol`: the 12 block columns of row i are distinct, include i, and each lies within cyclic distance 8 of i modulo 4096. `ocol`: the 12 block columns of row i are distinct, include i, and each lies within cyclic distance 8 of i modulo 4096.
All inputs are finite; a program needn't handle non-finite values.
Results may differ from a plain program's by a relative error of at most 0.0049.
Values may be sent and summed in bfloat16 or wider, within the bound.
No kernel may reach another device: no remote copies, remote signals or barrier semaphores. Data moves between devices by JAX's collectives and lax.ppermute only.
A program may use at most 64 MiB of HBM per device.

v0:
```python
import jax
import jax.numpy as jnp
from jax import lax
from jax.sharding import PartitionSpec as P


def with_halo(cells, sides, width):
    for axis, dim in sides:
        count = lax.axis_size(axis)
        head = lax.slice_in_dim(cells, 0, width, axis=dim)
        tail = lax.slice_in_dim(cells, cells.shape[dim] - width, cells.shape[dim], axis=dim)
        cells = jnp.concatenate(
            [
                lax.ppermute(tail, axis, [(i, (i + 1) % count) for i in range(count)]),
                cells,
                lax.ppermute(head, axis, [((i + 1) % count, i) for i in range(count)]),
            ],
            axis=dim,
        )
    return cells


def per_device(tval, tcol, ocol, basis):
    local = tval.shape[0]
    size = tval.shape[2]
    width = basis.shape[1]
    slots = tval.shape[1]
    devices = lax.axis_size(("wide", "narrow"))
    count = local * devices
    first = lax.axis_index(("wide", "narrow")) * local
    extended = with_halo(tval, ((("wide", "narrow"), 0),), local)
    basis_ext = with_halo(basis, ((("wide", "narrow"), 0),), local * size)
    basis_blocks = basis_ext.reshape(3 * local, size, width)
    slot_ids = jnp.arange(slots, dtype=jnp.int32)

    def one_row(index):
        glob = first + index
        cols = tcol[glob]
        places = (cols - first + local) % count
        pattern = tcol[cols]
        outcols = ocol[index]
        match = (pattern[None, :, :] == outcols[:, None, None]).astype(jnp.int32)
        which = jnp.sum(match * slot_ids[None, None, :], axis=2)
        valid = jnp.sum(match, axis=2).astype(jnp.bfloat16)
        chosen = extended[places[None, :], which]
        selected = chosen * valid[:, :, None, None]
        square = jnp.einsum(
            "sab,osbc->oac", tval[index], selected, preferred_element_type=jnp.float32
        ).astype(jnp.bfloat16)
        picked = basis_blocks[(outcols - first + local) % count]
        result = jnp.einsum("oac,ock->ak", square, picked, preferred_element_type=jnp.float32)
        return result.astype(jnp.bfloat16)

    projected = lax.map(one_row, jnp.arange(local, dtype=jnp.int32)).reshape(local * size, width)
    partial_level = jnp.dot(basis.T, projected, preferred_element_type=jnp.float32)
    level = lax.psum(partial_level, ("wide", "narrow"))
    level = level / jnp.sqrt(jnp.float32(count * size))
    return (projected, level)


def solution(mesh):
    return jax.shard_map(
        per_device,
        mesh=mesh,
        in_specs=(
            P(("wide", "narrow"), None, None, None),
            P(),
            P(("wide", "narrow"), None),
            P(("wide", "narrow"), None),
        ),
        out_specs=(P(("wide", "narrow"), None), P()),
        check_vma=False,
    )
```

profile of v0, /device:TPU:1, one launch (start us, length us, event | category | flops | bytes accessed | tf_op | source)
XLA Modules:
  0.0 650.9 jit_solution(2711179265260050932)
XLA Ops:
  7.2 7.2 %collective-permute-start = (bf16[8,12,128,128]{3,2,1,0:T(8,128)(2,1)}, bf16[8,12,128,128]{3,2,1,0:T(8,128)(2,1)}, u32[]{:S(2)}, u32[]{:S(2)}) collective-permute-start(bf16[8,12,128,128]{3,2,1,0:T(8,128)(2,1)} %param.6), channel_id=1, source_target_pairs={{0,1},{1,2},{2,3},{3,4},{4,5},{5,6},{6,7},{7,8},{8,9},{9,10},{10,1... | collective-permute-start | bytes 9437192 | tf_op jit(solution)/shard_map/ppermute | solution.py:14
  14.4 3.5 collective-permute-start.1
  17.9 3.0 collective-permute-start.2
  20.9 9.1 %collective-permute-start.3 = (bf16[1024,128]{1,0:T(8,128)(2,1)}, bf16[1024,128]{1,0:T(8,128)(2,1)S(1)}, u32[]{:S(2)}, u32[]{:S(2)}) collective-permute-start(bf16[1024,128]{1,0:T(8,128)(2,1)} %param.9), channel_id=1, source_target_pairs={{1,0},{2,1},{3,2},{4,3},{5,4},{6,5},{7,6},{8,7},{9,8},{10,9},{11,1... | collective-permute-start | bytes 786440 | tf_op jit(solution)/shard_map/ppermute | solution.py:16
  30.0 1.6 copy.12
  31.6 55.9 %collective-permute-done.2 = bf16[1024,128]{1,0:T(8,128)(2,1)S(1)} collective-permute-done((bf16[1024,128]{1,0:T(8,128)(2,1)}, bf16[1024,128]{1,0:T(8,128)(2,1)S(1)}, u32[]{:S(2)}, u32[]{:S(2)}) %collective-permute-start.2) | collective-permute-done | bytes 262176 | tf_op jit(solution)/shard_map/ppermute | solution.py:14
  87.5 6.0 collective-permute-done.3
  93.5 1.0 pad_maximum_fusion.1
  94.5 7.7 %pad_maximum_fusion = bf16[24,12,128,128]{3,2,1,0:T(8,128)(2,1)} fusion(bf16[8,12,128,128]{3,2,1,0:T(8,128)(2,1)} %collective-permute-done.1, bf16[8,12,128,128]{3,2,1,0:T(8,128)(2,1)} %param.6, bf16[8,12,128,128]{3,2,1,0:T(8,128)(2,1)} %collective-permute-done), kind=kLoop, calls=%fused_computation.47 | loop fusion | flops 9437184 | bytes 18874368 | tf_op jit(solution)/shard_map/concatenate | solution.py:12
  102.2 269.6 %while.13 = (s32[]{:T(128)}, bf16[8,128,128]{2,1,0:T(8,128)(2,1)}, s32[8]{0:T(128)S(1)}, s32[]{:T(128)}, s32[4096,12]{1,0:T(8,128)S(1)}, /*index=5*/s32[8,12]{1,...) while((s32[]{:T(128)}, bf16[8,128,128]{2,1,0:T(8,128)(2,1)}, ...), condition=%wide.region_3.4_spmd.clone, body=%wide.region_0.3_spmd.clone.sunk | while | flops 656895552 | bytes 25215700 | solution.py:54
  105.4 0.7 fusion.62
  106.6 0.7 fusion.63
  108.0 15.8 %gather_fusion.2 = bf16[144,128,128]{2,1,0:T(8,128)(2,1)} fusion(bf16[24,12,128,128]{3,2,1,0:T(8,128)(2,1)} %get-tuple-element.305, s32[144]{0:T(256)S(1)} %reshape.191), kind=kCustom, calls=%fused_computation.1.clone.clone.1 | custom fusion | bytes 9438336 | tf_op jit(solution)/shard_map/while/body/eval_jaxpr/gather | solution.py:45
  123.8 6.7 %copy.17 = bf16[12,12,128,128]{2,3,1,0:T(8,128)(2,1)} copy(bf16[12,12,128,128]{3,2,1,0:T(8,128)(2,1)} %bitcast.95) | data formatting | bytes 9437184 | tf_op jit(solution)/shard_map/while/body/eval_jaxpr/gather | solution.py:45
  131.1 4.8 fusion.66
  140.3 0.7 fusion.63
  141.7 15.8 %gather_fusion.2 = bf16[144,128,128]{2,1,0:T(8,128)(2,1)} fusion(bf16[24,12,128,128]{3,2,1,0:T(8,128)(2,1)} %get-tuple-element.305, s32[144]{0:T(256)S(1)} %reshape.191), kind=kCustom, calls=%fused_computation.1.clone.clone.1 | custom fusion | bytes 9438336 | tf_op jit(solution)/shard_map/while/body/eval_jaxpr/gather | solution.py:45
  157.5 6.7 %copy.17 = bf16[12,12,128,128]{2,3,1,0:T(8,128)(2,1)} copy(bf16[12,12,128,128]{3,2,1,0:T(8,128)(2,1)} %bitcast.95) | data formatting | bytes 9437184 | tf_op jit(solution)/shard_map/while/body/eval_jaxpr/gather | solution.py:45
  164.8 4.8 fusion.66
  174.0 0.7 fusion.63
  175.4 15.8 %gather_fusion.2 = bf16[144,128,128]{2,1,0:T(8,128)(2,1)} fusion(bf16[24,12,128,128]{3,2,1,0:T(8,128)(2,1)} %get-tuple-element.305, s32[144]{0:T(256)S(1)} %reshape.191), kind=kCustom, calls=%fused_computation.1.clone.clone.1 | custom fusion | bytes 9438336 | tf_op jit(solution)/shard_map/while/body/eval_jaxpr/gather | solution.py:45
  191.2 6.7 %copy.17 = bf16[12,12,128,128]{2,3,1,0:T(8,128)(2,1)} copy(bf16[12,12,128,128]{3,2,1,0:T(8,128)(2,1)} %bitcast.95) | data formatting | bytes 9437184 | tf_op jit(solution)/shard_map/while/body/eval_jaxpr/gather | solution.py:45
  198.5 4.8 fusion.66
  207.7 0.7 fusion.63
  209.1 15.8 %gather_fusion.2 = bf16[144,128,128]{2,1,0:T(8,128)(2,1)} fusion(bf16[24,12,128,128]{3,2,1,0:T(8,128)(2,1)} %get-tuple-element.305, s32[144]{0:T(256)S(1)} %reshape.191), kind=kCustom, calls=%fused_computation.1.clone.clone.1 | custom fusion | bytes 9438336 | tf_op jit(solution)/shard_map/while/body/eval_jaxpr/gather | solution.py:45
  224.9 6.7 %copy.17 = bf16[12,12,128,128]{2,3,1,0:T(8,128)(2,1)} copy(bf16[12,12,128,128]{3,2,1,0:T(8,128)(2,1)} %bitcast.95) | data formatting | bytes 9437184 | tf_op jit(solution)/shard_map/while/body/eval_jaxpr/gather | solution.py:45
  232.2 4.8 fusion.66
  241.4 0.7 fusion.63
  242.8 15.8 %gather_fusion.2 = bf16[144,128,128]{2,1,0:T(8,128)(2,1)} fusion(bf16[24,12,128,128]{3,2,1,0:T(8,128)(2,1)} %get-tuple-element.305, s32[144]{0:T(256)S(1)} %reshape.191), kind=kCustom, calls=%fused_computation.1.clone.clone.1 | custom fusion | bytes 9438336 | tf_op jit(solution)/shard_map/while/body/eval_jaxpr/gather | solution.py:45
  258.6 6.7 %copy.17 = bf16[12,12,128,128]{2,3,1,0:T(8,128)(2,1)} copy(bf16[12,12,128,128]{3,2,1,0:T(8,128)(2,1)} %bitcast.95) | data formatting | bytes 9437184 | tf_op jit(solution)/shard_map/while/body/eval_jaxpr/gather | solution.py:45
  265.9 4.8 fusion.66
  273.8 0.7 fusion.62
  275.1 0.7 fusion.63
  276.5 15.8 %gather_fusion.2 = bf16[144,128,128]{2,1,0:T(8,128)(2,1)} fusion(bf16[24,12,128,128]{3,2,1,0:T(8,128)(2,1)} %get-tuple-element.305, s32[144]{0:T(256)S(1)} %reshape.191), kind=kCustom, calls=%fused_computation.1.clone.clone.1 | custom fusion | bytes 9438336 | tf_op jit(solution)/shard_map/while/body/eval_jaxpr/gather | solution.py:45
  292.3 6.7 %copy.17 = bf16[12,12,128,128]{2,3,1,0:T(8,128)(2,1)} copy(bf16[12,12,128,128]{3,2,1,0:T(8,128)(2,1)} %bitcast.95) | data formatting | bytes 9437184 | tf_op jit(solution)/shard_map/while/body/eval_jaxpr/gather | solution.py:45
  299.7 4.8 fusion.66
  308.8 0.7 fusion.63
  310.2 15.8 %gather_fusion.2 = bf16[144,128,128]{2,1,0:T(8,128)(2,1)} fusion(bf16[24,12,128,128]{3,2,1,0:T(8,128)(2,1)} %get-tuple-element.305, s32[144]{0:T(256)S(1)} %reshape.191), kind=kCustom, calls=%fused_computation.1.clone.clone.1 | custom fusion | bytes 9438336 | tf_op jit(solution)/shard_map/while/body/eval_jaxpr/gather | solution.py:45
  326.1 6.7 %copy.17 = bf16[12,12,128,128]{2,3,1,0:T(8,128)(2,1)} copy(bf16[12,12,128,128]{3,2,1,0:T(8,128)(2,1)} %bitcast.95) | data formatting | bytes 9437184 | tf_op jit(solution)/shard_map/while/body/eval_jaxpr/gather | solution.py:45
  333.4 4.8 fusion.66
  342.6 0.7 fusion.63
  343.9 15.8 %gather_fusion.2 = bf16[144,128,128]{2,1,0:T(8,128)(2,1)} fusion(bf16[24,12,128,128]{3,2,1,0:T(8,128)(2,1)} %get-tuple-element.305, s32[144]{0:T(256)S(1)} %reshape.191), kind=kCustom, calls=%fused_computation.1.clone.clone.1 | custom fusion | bytes 9438336 | tf_op jit(solution)/shard_map/while/body/eval_jaxpr/gather | solution.py:45
  359.8 6.7 %copy.17 = bf16[12,12,128,128]{2,3,1,0:T(8,128)(2,1)} copy(bf16[12,12,128,128]{3,2,1,0:T(8,128)(2,1)} %bitcast.95) | data formatting | bytes 9437184 | tf_op jit(solution)/shard_map/while/body/eval_jaxpr/gather | solution.py:45
  367.1 4.8 fusion.66
  371.9 1.9 convolution_bitcast_fusion
  373.7 268.7 %all-reduce.2.cloned.1.call-done = f32[128,128]{0,1:T(8,128)} async-done(((f32[128,128]{0,1:T(8,128)}), f32[128,128]{0,1:T(8,128)}) %all-reduce.2.cloned.1.call-update) | async-done | bytes 65552 | tf_op jit(solution)/shard_map/psum | solution.py:56
  642.5 0.8 broadcast_multiply_fusion
  643.3 0.7 copy.13
  (86 shorter events, 24.0 us)
Async XLA Ops:
  7.2 635.3 %all-reduce.2.cloned.1.call-start = ((), (), s32[]{:S(2)}) async-start(), calls=%async_computation | async-start | bytes 131072 | tf_op jit(solution)/shard_map/psum | solution.py:56
  7.2 87.3 %collective-permute-start = (bf16[8,12,128,128]{3,2,1,0:T(8,128)(2,1)}, bf16[8,12,128,128]{3,2,1,0:T(8,128)(2,1)}, u32[]{:S(2)}, u32[]{:S(2)}) collective-permute-start(bf16[8,12,128,128]{3,2,1,0:T(8,128)(2,1)} %param.6), channel_id=1, source_target_pairs={{0,1},{1,2},{2,3},{3,4},{4,5},{5,6},{6,7},{7,8},{8,9},{9,10},{10,1... | collective-permute-start | bytes 9437192 | tf_op jit(solution)/shard_map/ppermute | solution.py:14
  14.4 80.1 %collective-permute-start.1 = (bf16[8,12,128,128]{3,2,1,0:T(8,128)(2,1)}, bf16[8,12,128,128]{3,2,1,0:T(8,128)(2,1)}, u32[]{:S(2)}, u32[]{:S(2)}) collective-permute-start(bf16[8,12,128,128]{3,2,1,0:T(8,128)(2,1)} %param.6), channel_id=1, source_target_pairs={{1,0},{2,1},{3,2},{4,3},{5,4},{6,5},{7,6},{8,7},{9,8},{10,9},{11,1... | collective-permute-start | bytes 9437192 | tf_op jit(solution)/shard_map/ppermute | solution.py:16
  17.9 69.6 %collective-permute-start.2 = (bf16[1024,128]{1,0:T(8,128)(2,1)}, bf16[1024,128]{1,0:T(8,128)(2,1)S(1)}, u32[]{:S(2)}, u32[]{:S(2)}) collective-permute-start(bf16[1024,128]{1,0:T(8,128)(2,1)} %param.9), channel_id=1, source_target_pairs={{0,1},{1,2},{2,3},{3,4},{4,5},{5,6},{6,7},{7,8},{8,9},{9,10},{10,1... | collective-permute-start | bytes 786440 | tf_op jit(solution)/shard_map/ppermute | solution.py:14
  20.9 72.6 %collective-permute-start.3 = (bf16[1024,128]{1,0:T(8,128)(2,1)}, bf16[1024,128]{1,0:T(8,128)(2,1)S(1)}, u32[]{:S(2)}, u32[]{:S(2)}) collective-permute-start(bf16[1024,128]{1,0:T(8,128)(2,1)} %param.9), channel_id=1, source_target_pairs={{1,0},{2,1},{3,2},{4,3},{5,4},{6,5},{7,6},{8,7},{9,8},{10,9},{11,1... | collective-permute-start | bytes 786440 | tf_op jit(solution)/shard_map/ppermute | solution.py:16
  102.2 269.6 %copy-start = (bf16[1024,128]{1,0:T(8,128)(2,1)S(1)}, bf16[1024,128]{1,0:T(8,128)(2,1)}, u32[]{:S(2)}) copy-start(bf16[1024,128]{1,0:T(8,128)(2,1)} %param.9) | copy-start | bytes 786436
Sparse Core Ops, SparseCore 0:
  373.8 268.5 all-reduce.1
where the time goes:
time: 653 us; the launch traced here: 651 us
  waiting for transfers between devices  331 us (51%)
  local copies, waits for them, and re-layouts  197 us (30%)
  matrix products  40 us (6%)
  other arithmetic  25.5 us (4%)
  starting transfers between devices  22.8 us (3%)
  loops' own time  20.3 us (3%)
  between operations  14.1 us (2%)
    psum x1, waiting for transfers between devices, per_device(): level = lax.psum(partial_level, ('wide', 'narrow'))  269 us
    gather x16, local copies, waits for them, and re-layouts, one_row(): chosen = extended[places[None, :], which]  180 us
    ppermute x2, waiting for transfers between devices, with_halo(): lax.ppermute(tail, axis, [(i, (i + 1) % count) for i in range(count)])  55.9 us
    dot_general x8, matrix products, one_row(): jnp.einsum('oac,ock->ak', square, picked, preferred_element_type=jnp.floa...  38.2 us
    another operation x1, loops' own time, per_device(): lax.map(one_row, jnp.arange(local, dtype=jnp.int32))  20.3 us
  transfers between devices with their start and end apart: 5, of which 3 were waited for; matrix products, arithmetic and copies ran while one was open for 0% of the time, Pallas kernels for 0%

commit v1 on v0

--- a/solution.py
+++ b/solution.py
@@ -53,7 +53,7 @@
 
     projected = lax.map(one_row, jnp.arange(local, dtype=jnp.int32)).reshape(local * size, width)
     partial_level = jnp.dot(basis.T, projected, preferred_element_type=jnp.float32)
-    level = lax.psum(partial_level, ("wide", "narrow"))
+    level = lax.psum(lax.psum(partial_level, "narrow"), "wide")
     level = level / jnp.sqrt(jnp.float32(count * size))
     return (projected, level)
 

time: 653 us -> 1000 us (1.53)
  the two profiles are of different devices: /device:TPU:1 before, /device:TPU:70 now
where the time goes in v1:
time: 1000 us
  waiting for transfers between devices  685 us (68%)
  local copies, waits for them, and re-layouts  197 us (20%)
  matrix products  40 us (4%)
  other arithmetic  25.5 us (3%)
  loops' own time  20.3 us (2%)
  starting transfers between devices  20 us (2%)
  between operations  14.1 us (1%)
    psum x2, waiting for transfers between devices, per_device(): level = lax.psum(lax.psum(partial_level, 'narrow'), 'wide')  611 us
    gather x16, local copies, waits for them, and re-layouts, one_row(): chosen = extended[places[None, :], which]  180 us
    ppermute x2, waiting for transfers between devices, with_halo(): lax.ppermute(tail, axis, [(i, (i + 1) % count) for i in range(count)])  73.8 us
    dot_general x8, matrix products, one_row(): jnp.einsum('oac,ock->ak', square, picked, preferred_element_type=jnp.floa...  38.2 us
    another operation x1, loops' own time, per_device(): lax.map(one_row, jnp.arange(local, dtype=jnp.int32))  20.3 us
  transfers between devices with their start and end apart: 6, of which 3 were waited for; matrix products, arithmetic and copies ran while one was open for 0% of the time, Pallas kernels for 0%

profile of v1, /device:TPU:70, one launch (start us, length us, event | category | flops | bytes accessed | tf_op | source)
XLA Modules:
  0.0 1002.5 jit_solution(6534565014307304934)
XLA Ops:
  7.2 1.9 collective-permute-start
  9.1 9.5 collective-permute-start.1
  18.6 1.9 collective-permute-start.2
  20.5 6.7 collective-permute-start.3
  27.2 1.6 copy.12
  28.8 73.8 %collective-permute-done.2 = bf16[1024,128]{1,0:T(8,128)(2,1)S(1)} collective-permute-done((bf16[1024,128]{1,0:T(8,128)(2,1)}, bf16[1024,128]{1,0:T(8,128)(2,1)S(1)}, u32[]{:S(2)}, u32[]{:S(2)}) %collective-permute-start.2) | collective-permute-done | bytes 262176 | tf_op jit(solution)/shard_map/ppermute | solution.py:14
  102.6 1.0 pad_maximum_fusion.1
  103.7 7.7 pad_maximum_fusion
  111.4 269.6 %while.13 = (s32[]{:T(128)}, bf16[8,128,128]{2,1,0:T(8,128)(2,1)}, s32[8]{0:T(128)S(1)}, s32[]{:T(128)}, s32[4096,12]{1,0:T(8,128)S(1)}, /*index=5*/s32[8,12]{1,...) while((s32[]{:T(128)}, bf16[8,128,128]{2,1,0:T(8,128)(2,1)}, ...), condition=%wide.region_3.4_spmd.clone, body=%wide.region_0.3_spmd.clone.sunk | while | flops 656895552 | bytes 25215700 | solution.py:54
  115.8 0.7 fusion.63
  117.1 15.8 %gather_fusion.2 = bf16[144,128,128]{2,1,0:T(8,128)(2,1)} fusion(bf16[24,12,128,128]{3,2,1,0:T(8,128)(2,1)} %get-tuple-element.305, s32[144]{0:T(256)S(1)} %reshape.191), kind=kCustom, calls=%fused_computation.1.clone.clone.1 | custom fusion | bytes 9438336 | tf_op jit(solution)/shard_map/while/body/eval_jaxpr/gather | solution.py:45
  132.9 6.7 copy.17
  140.3 4.8 fusion.66
  149.4 0.7 fusion.63
  150.8 15.8 %gather_fusion.2 = bf16[144,128,128]{2,1,0:T(8,128)(2,1)} fusion(bf16[24,12,128,128]{3,2,1,0:T(8,128)(2,1)} %get-tuple-element.305, s32[144]{0:T(256)S(1)} %reshape.191), kind=kCustom, calls=%fused_computation.1.clone.clone.1 | custom fusion | bytes 9438336 | tf_op jit(solution)/shard_map/while/body/eval_jaxpr/gather | solution.py:45
  166.6 6.7 copy.17
  174.0 4.8 fusion.66
  183.1 0.7 fusion.63
  184.5 15.8 %gather_fusion.2 = bf16[144,128,128]{2,1,0:T(8,128)(2,1)} fusion(bf16[24,12,128,128]{3,2,1,0:T(8,128)(2,1)} %get-tuple-element.305, s32[144]{0:T(256)S(1)} %reshape.191), kind=kCustom, calls=%fused_computation.1.clone.clone.1 | custom fusion | bytes 9438336 | tf_op jit(solution)/shard_map/while/body/eval_jaxpr/gather | solution.py:45
  200.4 6.7 copy.17
  207.7 4.8 fusion.66
  216.8 0.7 fusion.63
  218.2 15.8 %gather_fusion.2 = bf16[144,128,128]{2,1,0:T(8,128)(2,1)} fusion(bf16[24,12,128,128]{3,2,1,0:T(8,128)(2,1)} %get-tuple-element.305, s32[144]{0:T(256)S(1)} %reshape.191), kind=kCustom, calls=%fused_computation.1.clone.clone.1 | custom fusion | bytes 9438336 | tf_op jit(solution)/shard_map/while/body/eval_jaxpr/gather | solution.py:45
  234.1 6.7 copy.17
  241.4 4.8 fusion.66
  249.3 0.7 fusion.62
  250.6 0.7 fusion.63
  251.9 15.8 %gather_fusion.2 = bf16[144,128,128]{2,1,0:T(8,128)(2,1)} fusion(bf16[24,12,128,128]{3,2,1,0:T(8,128)(2,1)} %get-tuple-element.305, s32[144]{0:T(256)S(1)} %reshape.191), kind=kCustom, calls=%fused_computation.1.clone.clone.1 | custom fusion | bytes 9438336 | tf_op jit(solution)/shard_map/while/body/eval_jaxpr/gather | solution.py:45
  267.8 6.7 copy.17
  275.1 4.8 fusion.66
  284.3 0.7 fusion.63
  285.6 15.8 %gather_fusion.2 = bf16[144,128,128]{2,1,0:T(8,128)(2,1)} fusion(bf16[24,12,128,128]{3,2,1,0:T(8,128)(2,1)} %get-tuple-element.305, s32[144]{0:T(256)S(1)} %reshape.191), kind=kCustom, calls=%fused_computation.1.clone.clone.1 | custom fusion | bytes 9438336 | tf_op jit(solution)/shard_map/while/body/eval_jaxpr/gather | solution.py:45
  301.5 6.7 copy.17
  308.8 4.8 fusion.66
  318.0 0.7 fusion.63
  319.3 15.8 %gather_fusion.2 = bf16[144,128,128]{2,1,0:T(8,128)(2,1)} fusion(bf16[24,12,128,128]{3,2,1,0:T(8,128)(2,1)} %get-tuple-element.305, s32[144]{0:T(256)S(1)} %reshape.191), kind=kCustom, calls=%fused_computation.1.clone.clone.1 | custom fusion | bytes 9438336 | tf_op jit(solution)/shard_map/while/body/eval_jaxpr/gather | solution.py:45
  335.2 6.7 copy.17
  342.5 4.8 fusion.66
  350.4 0.7 fusion.62
  351.7 0.7 fusion.63
  353.1 15.8 %gather_fusion.2 = bf16[144,128,128]{2,1,0:T(8,128)(2,1)} fusion(bf16[24,12,128,128]{3,2,1,0:T(8,128)(2,1)} %get-tuple-element.305, s32[144]{0:T(256)S(1)} %reshape.191), kind=kCustom, calls=%fused_computation.1.clone.clone.1 | custom fusion | bytes 9438336 | tf_op jit(solution)/shard_map/while/body/eval_jaxpr/gather | solution.py:45
  368.9 6.7 copy.17
  376.2 4.8 fusion.66
  381.0 1.9 convolution_bitcast_fusion
  382.9 75.6 %all-reduce.3.cloned.1.call-done = f32[128,128]{0,1:T(8,128)} async-done(((f32[128,128]{0,1:T(8,128)}), f32[128,128]{0,1:T(8,128)}) %all-reduce.3.cloned.1.call-update) | async-done | bytes 65552 | tf_op jit(solution)/shard_map/psum | solution.py:56
  458.6 535.5 %all-reduce.5.cloned.1.call-done = f32[128,128]{0,1:T(8,128)} async-done(((f32[128,128]{0,1:T(8,128)}), f32[128,128]{0,1:T(8,128)}) %all-reduce.5.cloned.1.call-update) | async-done | bytes 65552 | tf_op jit(solution)/shard_map/psum | solution.py:56
  994.1 0.8 broadcast_multiply_fusion
  994.9 0.7 copy.13
  (89 shorter events, 24.1 us)
Async XLA Ops:
  7.2 451.4 %all-reduce.3.cloned.1.call-start = ((), (), s32[]{:S(2)}) async-start(), calls=%async_computation | async-start | bytes 131072 | tf_op jit(solution)/shard_map/psum | solution.py:56
  7.2 96.4 %collective-permute-start = (bf16[8,12,128,128]{3,2,1,0:T(8,128)(2,1)}, bf16[8,12,128,128]{3,2,1,0:T(8,128)(2,1)}, u32[]{:S(2)}, u32[]{:S(2)}) collective-permute-start(bf16[8,12,128,128]{3,2,1,0:T(8,128)(2,1)} %param.6), channel_id=1, source_target_pairs={{0,1},{1,2},{2,3},{3,4},{4,5},{5,6},{6,7},{7,8},{8,9},{9,10},{10,1... | collective-permute-start | bytes 9437192 | tf_op jit(solution)/shard_map/ppermute | solution.py:14
  9.1 94.5 %collective-permute-start.1 = (bf16[8,12,128,128]{3,2,1,0:T(8,128)(2,1)}, bf16[8,12,128,128]{3,2,1,0:T(8,128)(2,1)}, u32[]{:S(2)}, u32[]{:S(2)}) collective-permute-start(bf16[8,12,128,128]{3,2,1,0:T(8,128)(2,1)} %param.6), channel_id=1, source_target_pairs={{1,0},{2,1},{3,2},{4,3},{5,4},{6,5},{7,6},{8,7},{9,8},{10,9},{11,1... | collective-permute-start | bytes 9437192 | tf_op jit(solution)/shard_map/ppermute | solution.py:16
  18.6 84.0 %collective-permute-start.2 = (bf16[1024,128]{1,0:T(8,128)(2,1)}, bf16[1024,128]{1,0:T(8,128)(2,1)S(1)}, u32[]{:S(2)}, u32[]{:S(2)}) collective-permute-start(bf16[1024,128]{1,0:T(8,128)(2,1)} %param.9), channel_id=1, source_target_pairs={{0,1},{1,2},{2,3},{3,4},{4,5},{5,6},{6,7},{7,8},{8,9},{9,10},{10,1... | collective-permute-start | bytes 786440 | tf_op jit(solution)/shard_map/ppermute | solution.py:14
  20.5 82.1 %collective-permute-start.3 = (bf16[1024,128]{1,0:T(8,128)(2,1)}, bf16[1024,128]{1,0:T(8,128)(2,1)S(1)}, u32[]{:S(2)}, u32[]{:S(2)}) collective-permute-start(bf16[1024,128]{1,0:T(8,128)(2,1)} %param.9), channel_id=1, source_target_pairs={{1,0},{2,1},{3,2},{4,3},{5,4},{6,5},{7,6},{8,7},{9,8},{10,9},{11,1... | collective-permute-start | bytes 786440 | tf_op jit(solution)/shard_map/ppermute | solution.py:16
  111.4 269.6 %copy-start = (bf16[1024,128]{1,0:T(8,128)(2,1)S(1)}, bf16[1024,128]{1,0:T(8,128)(2,1)}, u32[]{:S(2)}) copy-start(bf16[1024,128]{1,0:T(8,128)(2,1)} %param.9) | copy-start | bytes 786436
  382.9 611.2 %all-reduce.5.cloned.1.call-start = ((), (), s32[]{:S(2)}) async-start(), calls=%async_computation.1 | async-start | bytes 131072 | tf_op jit(solution)/shard_map/psum | solution.py:56
Sparse Core Ops, SparseCore 0:
  383.0 75.5 all-reduce.2
  461.7 532.3 all-reduce.4
